TPU v7x, 256 devices: a whole 4x4x8 slice. The times are simulated.
256 devices in a mesh: row: 64 (over z, x, core), col: 4 (over y).
Axes of the slice: x: 4, y: 4, z: 8, core: 2. Of those that a mesh axis runs over, the one named last changes fastest.
Arguments:
- off_blocks: bfloat16 [16384, 4, 96, 96], P(('row', 'col')), may hold values from -0.625 to 0.625
- neighbour: int32 [16384, 4], P(('row', 'col')), may hold values from 0 to 5
- active: int32 [16384, 4], P(('row', 'col')), may hold values 0 or 1
- diag_blocks: bfloat16 [16384, 96, 96], P(('row', 'col')), may hold values from -0.625 to 0.625
- diag_inverse: bfloat16 [16384, 96, 96], P(('row', 'col')), may hold values from -0.625 to 0.625
- tentative: bfloat16 [16384, 96, 96], P(('row', 'col')), may hold values from -0.21875 to 0.21875
- aggregate: int32 [16384], P(('row', 'col')), may hold values from 0 to 1
- owner_row: int32 [2048, 1], P('row'), may hold values from 0 to 63; in each aligned block of 32 rows (0 to 31, 32 to 63, ...) at most 2 rows name the same one
- owner_group: int32 [2048], P('row'), may hold values from 0 to 7
Outputs:
- coarse_blocks: float32 [512, 192, 192], P('row', 'col')
Inputs may be any that keep to these rules, and one draw needn't show every extreme that they name: `owner_row`: among the 32 clusters of one row tile at most 2 have the same owner row, and exactly 2 do in some tile.
All inputs are finite; a program needn't handle non-finite values. No bound on the sum of `active` on one device may be relied on, other than what follows from the above.
Results may differ from a plain program's by a relative error of at most 0.006.
Values may be sent and summed in bfloat16 or wider, within the bound.
A program may use at most 128 MiB of HBM per device.

v0:
```python
import jax
import jax.numpy as jnp
from jax import lax
from jax.sharding import PartitionSpec as P

CW = 2
RQ = 2
G_DEV = 8


OMEGA = 0.6


def with_halo(block, sides, width):
    for axis, dim in sides:
        count = lax.axis_size(axis)
        forward = [(i, i + 1) for i in range(count - 1)]
        forward.append((count - 1, 0))
        backward = [(target, source) for source, target in forward]
        low = lax.ppermute(
            lax.slice_in_dim(block, block.shape[dim] - width, None, axis=dim), axis, forward
        )
        high = lax.ppermute(lax.slice_in_dim(block, 0, width, axis=dim), axis, backward)
        block = jnp.concatenate([low, block, high], axis=dim)
    return block


def widen(blocks, labels, window):
    onehot = (labels[..., None] == jnp.arange(window, dtype=jnp.int32)).astype(blocks.dtype)
    spread_out = blocks[..., :, None, :] * onehot[..., None, :, None]
    return spread_out.reshape(blocks.shape[:-1] + (window * blocks.shape[-1],))


def neighbour_index(near_slots, per_device):
    row_count = near_slots.shape[0]
    cluster_base = jnp.arange(row_count, dtype=jnp.int32) // per_device * per_device
    return near_slots // per_device * row_count + cluster_base[:, None] + near_slots % per_device


def apply_rows(diag_part, off_part, active_part, with_rim, near_index):
    row_count = diag_part.shape[0]
    own_rows = with_rim[row_count : 2 * row_count]
    near_rows = jnp.take(with_rim, near_index, axis=0)
    weights = off_part * active_part[:, :, None, None].astype(off_part.dtype)
    summed = jnp.einsum("rij,rjw->riw", diag_part, own_rows, preferred_element_type=jnp.float32)
    return summed + jnp.einsum(
        "rsij,rsjw->riw", weights, near_rows, preferred_element_type=jnp.float32
    )


def slot_table(target_row, group_labels, row_peers, capacity):
    cluster_count = target_row.shape[0]
    matches = (target_row[:, None] == jnp.arange(row_peers, dtype=jnp.int32)[None, :]).astype(
        jnp.int32
    )
    earlier = (jnp.arange(cluster_count)[:, None] > jnp.arange(cluster_count)[None, :]).astype(
        jnp.int32
    )
    before = jnp.sum(earlier[:, :, None] * matches[None, :, :], axis=1)
    position = jnp.sum(before * matches, axis=1)
    table = matches[:, :, None] * (
        position[:, None, None] == jnp.arange(capacity, dtype=jnp.int32)[None, None, :]
    ).astype(jnp.int32)
    slot_groups = jnp.sum(table * (group_labels + 1)[:, None, None], axis=0)
    return (table.astype(jnp.float32), slot_groups)


def collect(incoming, slot_groups):
    owned = (slot_groups[..., None] == jnp.arange(1, G_DEV + 1, dtype=jnp.int32)).astype(
        jnp.float32
    )
    return jnp.einsum("rcg,rcxy->gxy", owned, incoming, precision=lax.Precision.HIGHEST)


def on_device(
    off_blocks,
    neighbour,
    active,
    diag_blocks,
    diag_inverse,
    tentative,
    aggregate,
    owner_row,
    owner_group,
):
    row_count = diag_blocks.shape[0]
    near_index = neighbour_index(neighbour, RQ)
    tent_wide = widen(tentative, aggregate, CW)
    tent_rim = with_halo(tent_wide, (("col", 0),), row_count)
    smooth_in = apply_rows(diag_blocks, off_blocks, active, tent_rim, near_index).astype(
        jnp.bfloat16
    )
    correction = jnp.einsum(
        "rij,rjw->riw", diag_inverse, smooth_in, preferred_element_type=jnp.float32
    )
    prolong = (tent_wide.astype(jnp.float32) - OMEGA * correction).astype(jnp.bfloat16)
    prolong_rim = with_halo(prolong, (("col", 0),), row_count)
    stiff_prol = apply_rows(diag_blocks, off_blocks, active, prolong_rim, near_index).astype(
        jnp.bfloat16
    )
    clusters = owner_row.shape[0]
    window = prolong.shape[2]
    left_side = prolong.reshape(clusters, row_count // clusters * prolong.shape[1], window)
    right_side = stiff_prol.reshape(clusters, row_count // clusters * prolong.shape[1], window)
    partial_value = jnp.einsum(
        "qmx,qmy->qxy", left_side, right_side, preferred_element_type=jnp.float32
    )
    row_peers = lax.axis_size("row")
    capacity = max(2, 2 * clusters // row_peers)
    table, slot_groups = slot_table(owner_row[:, 0], owner_group, row_peers, capacity)
    row_shares = lax.psum_scatter(partial_value, "col", scatter_dimension=1, tiled=True)
    outgoing = jnp.einsum("qrc,qxy->rcxy", table, row_shares, precision=lax.Precision.HIGHEST)
    incoming, arrived = (
        lax.all_to_all(outgoing, "row", split_axis=0, concat_axis=0, tiled=True),
        lax.all_to_all(slot_groups, "row", split_axis=0, concat_axis=0, tiled=True),
    )
    return collect(incoming, arrived)


def solution(mesh):
    return jax.shard_map(
        on_device,
        mesh=mesh,
        in_specs=(
            P(("row", "col"), None, None, None),
            P(("row", "col"), None),
            P(("row", "col"), None),
            P(("row", "col"), None, None),
            P(("row", "col"), None, None),
            P(("row", "col"), None, None),
            P(("row", "col")),
            P("row", None),
            P("row"),
        ),
        out_specs=P("row", "col", None),
        check_vma=False,
    )
```

profile of v0, /device:TPU:1, one launch (start us, length us, event | category | flops | bytes accessed | tf_op | source)
XLA Modules:
  0.0 504.4 jit_solution(14414174962244202974)
XLA Ops:
  6.5 0.0 copy-start
  6.5 0.0 copy-start.7
  6.5 0.0 reduce-scatter.2.cloned.1.call-start
  6.5 6.5 %mul.101 = bf16[64,96,2,96]{3,2,1,0:T(2,128)(2,1)} broadcast(bf16[64,96,96]{2,1,0:T(8,128)(2,1)} %param.16), dimensions={0,1,3} | broadcast | bytes 3538944 | tf_op jit(solution)/shard_map/mul | solution.py:30
  13.0 0.0 copy-start.6
  13.0 0.0 copy-start.5
  13.0 6.0 %mul.102 = bf16[64,96,192]{2,1,0:T(8,128)(2,1)} reshape(bf16[64,96,2,96]{3,2,1,0:T(2,128)(2,1)} %mul.101) | data formatting | bytes 4718592 | tf_op jit(solution)/shard_map/mul | solution.py:30
  19.0 0.0 copy-done.7
  19.0 0.1 fusion.36
  19.1 0.1 mul.103
  19.2 0.1 mul.104
  19.3 3.8 broadcast_multiply_fusion
  23.1 2.1 collective-permute-start
  25.2 1.7 collective-permute-start.1
  26.9 0.0 copy-done.6
  27.0 0.1 copy.40
  27.1 0.1 reshape.163
  27.2 0.1 copy.39
  27.3 0.0 copy-done.5
  27.3 0.1 copy.38
  27.4 65.3 %collective-permute-done = bf16[64,96,192]{2,1,0:T(8,128)(2,1)} collective-permute-done((bf16[64,96,192]{2,1,0:T(8,128)(2,1)}, bf16[64,96,192]{2,1,0:T(8,128)(2,1)}, u32[]{:S(2)}, u32[]{:S(2)}) %collective-permute-start) | collective-permute-done | bytes 2359328 | tf_op jit(solution)/shard_map/ppermute | solution.py:20
  92.8 1.5 collective-permute-done.1
  94.3 8.2 %pad_maximum_fusion = bf16[192,96,192]{2,1,0:T(8,128)(2,1)} fusion(bf16[64,96,192]{2,1,0:T(8,128)(2,1)} %collective-permute-done.1, bf16[64,96,192]{2,1,0:T(8,128)(2,1)} %broadcast_multiply_fusion, bf16[64,96,192]{2,1,0:T(8,128)(2,1)} %collective-permute-done), kind=kLoop, calls=%fused_computation.8 | loop fusion | flops 7077888 | bytes 14155776 | tf_op jit(solution)/shard_map/concatenate | solution.py:24
  102.5 14.2 %gather_fusion = bf16[256,96,192]{2,1,0:T(8,128)(2,1)} fusion(bf16[192,96,192]{2,1,0:T(8,128)(2,1)} %pad_maximum_fusion, s32[1024]{0:T(1024)S(1)} %pad_clamp_fusion), kind=kCustom, calls=%fused_computation.clone | custom fusion | bytes 18875392 | tf_op jit(solution)/shard_map/jit(_take)/gather | solution.py:43
  116.7 0.0 copy-start.3
  116.7 10.7 %fusion.2 = f32[64,96,192,1]{1,2,3,0:T(8,128)} fusion(bf16[64,4,96,192]{3,2,1,0:T(8,128)(2,1)} %bitcast.53, pred[64,4]{1,0:T(8,128)(4,1)S(1)} %copy.39, bf16[64,4,96,96]{3,2,1,0:T(8,128)(2,1)} %param.11, bf16[64,4]{1,0:T(8,128)(2,1)S(1)} %copy.38), kind=kOutput, calls=%fused_computation.4 | convolution fusion | flops 913047552 | bytes 18875136 | tf_op jit(solution)/shard_map/rsij,rsjw->riw/dot_general | solution.py:46
  127.4 0.0 copy-done
  127.4 0.0 copy-done.3
  127.4 9.6 %fusion.7 = bf16[64,96,192]{2,1,0:T(8,128)(2,1)} fusion(bf16[64,96,192]{2,1,0:T(8,128)(2,1)} %broadcast_multiply_fusion, bf16[64,96,96]{2,1,0:T(8,128)(2,1)S(1)} %copy-done.3, f32[64,96,192,1]{1,2,3,0:T(8,128)} %fusion.2, bf16[64,96,96]{2,1,0:T(8,128)(2,1)S(1)} %copy-done), kind=kOutput, calls=%fused_computation.13 | convolution fusion | flops 460062720 | bytes 11796480 | tf_op jit(solution)/shard_map/rij,rjw->riw/dot_general | solution.py:93
  137.1 0.0 copy-start.2
  137.1 1.5 collective-permute-start.2
  138.5 1.7 collective-permute-start.3
  140.2 5.6 %fusion.54 = f32[64,192,96]{1,2,0:T(8,128)} fusion(bf16[64,96,96]{2,1,0:T(8,128)(2,1)S(1)} %copy-done, bf16[64,96,192]{2,1,0:T(8,128)(2,1)} %fusion.7), kind=kOutput, calls=%fused_computation.74 | convolution fusion | flops 226492416 | bytes 8257536 | tf_op jit(solution)/shard_map/rij,rjw->riw/dot_general | solution.py:45
  145.8 60.2 %collective-permute-done.2 = bf16[64,96,192]{2,1,0:T(8,128)(2,1)S(1)} collective-permute-done((bf16[64,96,192]{2,1,0:T(8,128)(2,1)}, bf16[64,96,192]{2,1,0:T(8,128)(2,1)S(1)}, u32[]{:S(2)}, u32[]{:S(2)}) %collective-permute-start.2) | collective-permute-done | bytes 2359328 | tf_op jit(solution)/shard_map/ppermute | solution.py:20
  206.0 0.6 collective-permute-done.3
  206.7 0.0 copy-done.2
  206.7 4.7 pad_maximum_fusion.1
  211.4 14.2 %gather_fusion.1 = bf16[256,96,192]{2,1,0:T(8,128)(2,1)} fusion(bf16[192,96,192]{2,1,0:T(8,128)(2,1)} %pad_maximum_fusion.1, s32[1024]{0:T(1024)S(1)} %pad_clamp_fusion), kind=kCustom, calls=%fused_computation.1.clone | custom fusion | bytes 18875392 | tf_op jit(solution)/shard_map/jit(_take)/gather | solution.py:43
  225.6 13.8 %fusion.6 = bf16[64,96,192]{2,1,0:T(8,128)(2,1)} fusion(f32[64,192,96]{1,2,0:T(8,128)} %fusion.54, bf16[64,4,96,192]{3,2,1,0:T(8,128)(2,1)} %bitcast.52, pred[64,4]{1,0:T(8,128)(4,1)S(1)} %copy.39, bf16[64,4,96,96]{3,2,1,0:T(8,128)(2,1)} %param.11, bf16[64,4]{1,0:T(8,128)(2,1)S(1)} %copy.38), kind=kOutput, calls=%fused_computation.11 | convolution fusion | flops 915406848 | bytes 21234432 | tf_op jit(solution)/shard_map/rsij,rsjw->riw/dot_general | solution.py:46
  239.4 6.8 %fusion.53 = f32[32,192,192]{2,1,0:T(8,128)} fusion(bf16[32,192,192]{2,1,0:T(8,128)(2,1)} %bitcast.51, bf16[32,192,192]{2,1,0:T(8,128)(2,1)} %bitcast.54), kind=kOutput, calls=%fused_computation.73 | convolution fusion | flops 452984832 | bytes 9437184 | tf_op jit(solution)/shard_map/qmx,qmy->qxy/dot_general | solution.py:105
  246.2 0.0 copy-start.4
  246.2 0.0 copy-start.8
  246.2 0.0 reduce-scatter.2.cloned.1.call-update
  246.3 0.6 copy-done.4
  246.9 0.1 fusion.39
  247.0 0.2 multiply_reduce_fusion
  247.2 0.2 select_reduce_fusion
  247.4 0.0 copy-done.8
  247.4 0.1 fusion.33
  247.5 0.7 copy.35
  248.2 14.8 %all-to-all-start = ((s32[64,1,2]{2,1,0:T(1,128)}), s32[64,1,2]{2,1,0:T(1,128)S(1)}, u32[]{:S(2)}, u32[]{:S(2)}) async-start(s32[64,1,2]{2,1,0:T(1,128)} %copy.35), calls=%async_computation | async-start | bytes 65536 | tf_op jit(solution)/shard_map/all_to_all | solution.py:115
  263.0 55.1 %reduce-scatter.2.cloned.1.call-done = f32[32,48,192]{2,1,0:T(8,128)} async-done(((f32[32,192,192]{2,1,0:T(8,128)}), f32[32,48,192]{2,1,0:T(8,128)}) %reduce-scatter.2.cloned.1.call-update) | async-done | bytes 1179664 | tf_op jit(solution)/shard_map/reduce_scatter | solution.py:111
  318.1 10.1 %fusion.27 = f32[64,2,48,192]{3,0,2,1:T(8,128)} fusion(f32[32,48,192]{2,1,0:T(8,128)} %reduce-scatter.2.cloned.1.call-done, s32[32,2]{0,1:T(2,128)S(1)} %compare_convert_fusion, s32[32,64]{1,0:T(8,128)S(1)} %fusion.39), kind=kOutput, calls=%fused_computation.26 | convolution fusion | flops 452993024 | bytes 5906688 | tf_op jit(solution)/shard_map/qrc,qxy->rcxy/dot_general | solution.py:112
  328.2 10.3 %copy.47 = f32[64,2,48,192]{3,1,2,0:T(2,128)} copy(f32[64,2,48,192]{3,0,2,1:T(8,128)} %fusion.27) | data formatting | bytes 9437184 | tf_op jit(solution)/shard_map/qrc,qxy->rcxy/dot_general | solution.py:112
  338.5 0.0 all-to-all-done
  338.5 11.2 %all-to-all-start.1 = ((f32[64,2,48,192]{3,1,2,0:T(2,128)}), f32[64,2,48,192]{3,1,2,0:T(2,128)}, u32[]{:S(2)}, u32[]{:S(2)}) async-start(f32[64,2,48,192]{3,1,2,0:T(2,128)} %copy.47), calls=%async_computation.2 | async-start | bytes 12582912 | tf_op jit(solution)/shard_map/all_to_all | solution.py:114
  349.7 0.0 copy-start.1
  349.7 0.1 copy.36
  349.8 138.4 %all-to-all-done.1 = f32[64,2,48,192]{3,1,2,0:T(2,128)} async-done(((f32[64,2,48,192]{3,1,2,0:T(2,128)}), f32[64,2,48,192]{3,1,2,0:T(2,128)}, u32[]{:S(2)}, u32[]{:S(2)}) %all-to-all-start.1) | async-done | bytes 4718624 | tf_op jit(solution)/shard_map/all_to_all | solution.py:114
  488.2 8.2 %fusion.30 = f32[8,48,192]{2,0,1:T(8,128)S(1)} fusion(f32[64,2,48,192]{3,1,2,0:T(2,128)} %all-to-all-done.1, s32[64,2]{0,1:T(2,128)S(1)} %bitcast.55, s32[8]{0:T(128)S(1)} %iota_add_fusion), kind=kOutput, calls=%fused_computation.30 | convolution fusion | flops 113247232 | bytes 5014048 | tf_op jit(solution)/shard_map/rcg,rcxy->gxy/dot_general | solution.py:72
  496.4 0.9 copy.49
  497.3 0.0 copy-done.1
  (8 shorter events, 0.1 us)
Async XLA Ops:
  6.5 120.9 %copy-start = (bf16[64,96,96]{2,1,0:T(8,128)(2,1)S(1)}, bf16[64,96,96]{2,1,0:T(8,128)(2,1)}, u32[]{:S(2)}) copy-start(bf16[64,96,96]{2,1,0:T(8,128)(2,1)} %param.14) | copy-start | bytes 3538948
  6.5 12.5 %copy-start.7 = (s32[64]{0:T(128)S(1)}, s32[64]{0:T(128)}, u32[]{:S(2)}) copy-start(s32[64]{0:T(128)} %param.17) | copy-start | bytes 772
  6.5 311.6 %reduce-scatter.2.cloned.1.call-start = ((), (), s32[]{:S(2)}) async-start(), calls=%async_computation.3 | async-start | bytes 7864320 | tf_op jit(solution)/shard_map/reduce_scatter | solution.py:111
  13.0 13.9 %copy-start.6 = (s32[64,4]{0,1:T(4,128)S(1)}, s32[64,4]{0,1:T(4,128)}, u32[]{:S(2)}) copy-start(s32[64,4]{0,1:T(4,128)} %param.12) | copy-start | bytes 3076
  13.0 14.3 %copy-start.5 = (s32[64,4]{0,1:T(4,128)S(1)}, s32[64,4]{0,1:T(4,128)}, u32[]{:S(2)}) copy-start(s32[64,4]{0,1:T(4,128)} %param.13) | copy-start | bytes 3076
  23.1 69.7 %collective-permute-start = (bf16[64,96,192]{2,1,0:T(8,128)(2,1)}, bf16[64,96,192]{2,1,0:T(8,128)(2,1)}, u32[]{:S(2)}, u32[]{:S(2)}) collective-permute-start(bf16[64,96,192]{2,1,0:T(8,128)(2,1)} %broadcast_multiply_fusion), channel_id=1, source_target_pairs={{0,1},{1,2},{2,3},{3,0},{4,5},{5,6},{6,7},{7,4},{8,9},{9,10},{10,1... | collective-permute-start | bytes 7077896 | tf_op jit(solution)/shard_map/ppermute | solution.py:20
  25.2 69.1 %collective-permute-start.1 = (bf16[64,96,192]{2,1,0:T(8,128)(2,1)}, bf16[64,96,192]{2,1,0:T(8,128)(2,1)}, u32[]{:S(2)}, u32[]{:S(2)}) collective-permute-start(bf16[64,96,192]{2,1,0:T(8,128)(2,1)} %broadcast_multiply_fusion), channel_id=1, source_target_pairs={{1,0},{2,1},{3,2},{0,3},{5,4},{6,5},{7,6},{4,7},{9,8},{10,9},{11,1... | collective-permute-start | bytes 7077896 | tf_op jit(solution)/shard_map/ppermute | solution.py:23
  116.7 10.7 %copy-start.3 = (bf16[64,96,96]{2,1,0:T(8,128)(2,1)S(1)}, bf16[64,96,96]{2,1,0:T(8,128)(2,1)}, u32[]{:S(2)}) copy-start(bf16[64,96,96]{2,1,0:T(8,128)(2,1)} %param.15) | copy-start | bytes 3538948
  137.1 69.6 %copy-start.2 = (bf16[64,96,192]{2,1,0:T(8,128)(2,1)S(1)}, bf16[64,96,192]{2,1,0:T(8,128)(2,1)}, u32[]{:S(2)}) copy-start(bf16[64,96,192]{2,1,0:T(8,128)(2,1)} %fusion.7) | copy-start | bytes 7077892
  137.1 69.0 %collective-permute-start.2 = (bf16[64,96,192]{2,1,0:T(8,128)(2,1)}, bf16[64,96,192]{2,1,0:T(8,128)(2,1)S(1)}, u32[]{:S(2)}, u32[]{:S(2)}) collective-permute-start(bf16[64,96,192]{2,1,0:T(8,128)(2,1)} %fusion.7), channel_id=1, source_target_pairs={{0,1},{1,2},{2,3},{3,0},{4,5},{5,6},{6,7},{7,4},{8,9},{9,10},{10,1... | collective-permute-start | bytes 7077896 | tf_op jit(solution)/shard_map/ppermute | solution.py:20
  138.5 68.2 %collective-permute-start.3 = (bf16[64,96,192]{2,1,0:T(8,128)(2,1)}, bf16[64,96,192]{2,1,0:T(8,128)(2,1)S(1)}, u32[]{:S(2)}, u32[]{:S(2)}) collective-permute-start(bf16[64,96,192]{2,1,0:T(8,128)(2,1)} %fusion.7), channel_id=1, source_target_pairs={{1,0},{2,1},{3,2},{0,3},{5,4},{6,5},{7,6},{4,7},{9,8},{10,9},{11,1... | collective-permute-start | bytes 7077896 | tf_op jit(solution)/shard_map/ppermute | solution.py:23
  246.2 0.7 copy-start.4
  246.2 1.1 copy-start.8
  248.2 90.3 %all-to-all-start = ((s32[64,1,2]{2,1,0:T(1,128)}), s32[64,1,2]{2,1,0:T(1,128)S(1)}, u32[]{:S(2)}, u32[]{:S(2)}) async-start(s32[64,1,2]{2,1,0:T(1,128)} %copy.35), calls=%async_computation | async-start | bytes 65536 | tf_op jit(solution)/shard_map/all_to_all | solution.py:115
  338.5 149.7 %all-to-all-start.1 = ((f32[64,2,48,192]{3,1,2,0:T(2,128)}), f32[64,2,48,192]{3,1,2,0:T(2,128)}, u32[]{:S(2)}, u32[]{:S(2)}) async-start(f32[64,2,48,192]{3,1,2,0:T(2,128)} %copy.47), calls=%async_computation.2 | async-start | bytes 12582912 | tf_op jit(solution)/shard_map/all_to_all | solution.py:114
  349.7 147.6 %copy-start.1 = (bf16[64,96,96]{2,1,0:T(8,128)(2,1)S(1)}, bf16[64,96,96]{2,1,0:T(8,128)(2,1)}, u32[]{:S(2)}) copy-start(bf16[64,96,96]{2,1,0:T(8,128)(2,1)} %param.14) | copy-start | bytes 3538948
Sparse Core Ops, SparseCore 0:
  246.4 71.6 reduce-scatter.1
where the time goes:
time: 510 us; the launch traced here: 504 us
  waiting for transfers between devices  321 us (63%)
  matrix products  64.9 us (13%)
  local copies, waits for them, and re-layouts  54.2 us (11%)
  starting transfers between devices  33 us (6%)
  other arithmetic  17.3 us (3%)
  between operations  13.7 us (3%)
    all_to_all x1, waiting for transfers between devices, on_device(): lax.all_to_all(outgoing, 'row', split_axis=0, concat_axis=0, tiled=True)  138 us
    ppermute x2, waiting for transfers between devices, with_halo(): lax.ppermute(lax.slice_in_dim(block, block.shape[dim] - width, None, axis...  126 us
    reduce_scatter x1, waiting for transfers between devices, on_device(): lax.psum_scatter(partial_value, 'col', scatter_dimension=1, tiled=True)  55.1 us
    gather x2, local copies, waits for them, and re-layouts, apply_rows(): near_rows = jnp.take(with_rim, near_index, axis=0)  28.5 us
    dot_general x2, matrix products, apply_rows(): jnp.einsum('rsij,rsjw->riw', weights, near_rows, preferred_element_type=j...  24.5 us
    all_to_all x1, starting transfers between devices, on_device(): lax.all_to_all(slot_groups, 'row', split_axis=0, concat_axis=0, tiled=True)  14.8 us
    concatenate x2, other arithmetic, with_halo(): block = jnp.concatenate([low, block, high], axis=dim)  12.9 us
    mul x4, local copies, waits for them, and re-layouts, widen(): spread_out = blocks[..., :, None, :] * onehot[..., None, :, None]  12.7 us
  transfers between devices with their start and end apart: 7, of which 6 were waited for; matrix products, arithmetic and copies ran while one was open for 6% of the time, Pallas kernels for 0%

commit v1 on v0

v1 whole, which is shorter than its diff:
```python
import jax
import jax.numpy as jnp
from jax import lax
from jax.experimental import pallas as pl
from jax.experimental.pallas import tpu as pltpu
from jax.sharding import PartitionSpec as P

MESH = pl.DeviceIdType.MESH
F32 = jnp.float32
BF16 = jnp.bfloat16
B = 96
LANES = 128
OMEGA = 0.6
ROWS = 64
PAIRS = 16
PEERS = 64
PLANES = 48


def pack4(b0, b1, b2, b3):
    high = lax.broadcasted_iota(jnp.int32, b0.shape, 1) >= B
    return (
        jnp.where(high, pltpu.roll(b3, 96, 1), b0),
        jnp.where(high, pltpu.roll(b3, 64, 1), b1),
        jnp.where(high, pltpu.roll(b3, 32, 1), b2),
    )


def unpack_last(t0, t1, t2):
    lane = lax.broadcasted_iota(jnp.int32, t0.shape, 1)
    return jnp.where(
        lane < 32,
        pltpu.roll(t0, 32, 1),
        jnp.where(lane < 64, pltpu.roll(t1, 64, 1), pltpu.roll(t2, 96, 1)),
    )


def dot(a, b):
    return lax.dot_general(a, b, (((1,), (0,)), ((), ())), preferred_element_type=F32)


def galerkin_kernel(
    slot_ref,
    label_ref,
    off_hbm,
    diag_hbm,
    inv_hbm,
    tent_hbm,
    out_ref,
    off,
    diag,
    inv,
    tent,
    wide,
    send_label,
    near_label,
    send_t,
    near_t,
    own_p,
    send_p,
    near_p,
    rim,
    part,
    send_far,
    send_next,
    send_back,
    near_far,
    near_next,
    near_back,
    hold_next,
    hold_own,
    planes,
    load_sem,
    tent_sem,
    label_send,
    label_recv,
    t_send,
    t_recv,
    p_send,
    p_recv,
    c_send,
    c_recv,
):
    me = lax.axis_index("col")
    right, left = lax.rem(me + 1, 4), lax.rem(me + 3, 4)

    def loads(p):
        rows = pl.ds(p * 4, 4)
        return [
            pltpu.make_async_copy(off_hbm.at[rows], off.at[rows], load_sem.at[0, p]),
            pltpu.make_async_copy(diag_hbm.at[rows], diag.at[rows], load_sem.at[1, p]),
            pltpu.make_async_copy(inv_hbm.at[rows], inv.at[rows], load_sem.at[2, p]),
        ]

    def remote(src, dst, send_sem, recv_sem, col):
        return pltpu.make_async_remote_copy(
            src_ref=src,
            dst_ref=dst,
            send_sem=send_sem,
            recv_sem=recv_sem,
            device_id={"col": col},
            device_id_type=MESH,
        )

    tent_copy = pltpu.make_async_copy(tent_hbm, tent, tent_sem)
    tent_copy.start()

    @pl.loop(0, PAIRS)
    def _(p):
        for copy in loads(p):
            copy.start()

    barrier = pltpu.get_barrier_semaphore()
    for peer in (left, right):
        pl.semaphore_signal(barrier, inc=1, device_id={"col": peer}, device_id_type=MESH)
    send_label[...] = label_ref[...]
    rim[...] = jnp.zeros_like(rim)
    pl.semaphore_wait(barrier, 2)

    def label_copy(side):
        return remote(
            send_label, near_label.at[side], label_send.at[side], label_recv.at[side],
            right if side == 0 else left,
        )

    def t_copy(side, p):
        return remote(
            send_t.at[p], near_t.at[side, p], t_send.at[side, p], t_recv.at[side, p],
            right if side == 0 else left,
        )

    def p_copy(side, p):
        rows = pl.ds(p * 2, 2)
        return remote(
            send_p.at[rows], near_p.at[side, rows], p_send.at[side, p], p_recv.at[side, p],
            right if side == 0 else left,
        )

    for side in range(2):
        label_copy(side).start()
    tent_copy.wait()

    @pl.loop(0, PAIRS)
    def _(p):
        for e in range(4):
            wide[p * 4 + e, :, 0:B] = tent[p * 4 + e]
        tiles = pack4(*[wide[p * 4 + e].astype(F32) for e in range(4)])
        for t in range(3):
            send_t[p, t] = tiles[t].astype(BF16)
        for side in range(2):
            t_copy(side, p).start()

    for side in range(2):
        label_copy(side).wait_recv()

    def apply(row, near_base, own):
        total = dot(diag[row], rim[near_base + own])
        for s in range(4):
            total = total + dot(off[row, s], rim[near_base + slot_ref[row * 4 + s]])
        return total

    @pl.loop(0, PAIRS)
    def _(p):
        for side in range(2):
            t_copy(side, p).wait_recv()
        for copy in loads(p):
            copy.wait()

        def spread(e, position, block, label):
            zero = jnp.zeros_like(block)
            at = (e // 2) * 7 + position + e % 2
            rim[at, :, 0:LANES] = jnp.where(label == 0.0, block, zero).astype(BF16)
            rim[at, :, LANES : 2 * LANES] = jnp.where(label == 1.0, block, zero).astype(BF16)

        for side in range(2):
            tiles = [near_t[side, p, t].astype(F32) for t in range(3)]
            tiles.append(unpack_last(*tiles))
            for e in range(4):
                spread(e, 4 * side, tiles[e], near_label[side, pl.ds(p * 4 + e, 1), :])
        for e in range(4):
            spread(e, 2, wide[p * 4 + e].astype(F32), send_label[pl.ds(p * 4 + e, 1), :])

        for c in range(2):
            blocks = []
            for k in range(2):
                row = p * 4 + c * 2 + k
                smooth = apply(row, c * 7, 2 + k).astype(BF16)
                prolong = rim[c * 7 + 2 + k].astype(F32) - OMEGA * dot(inv[row], smooth)
                rounded = prolong.astype(BF16)
                own_p[row] = rounded
                back = rounded.astype(F32)
                blocks += [back[:, 0:LANES], back[:, LANES : 2 * LANES]]
            tiles = pack4(*blocks)
            for t in range(3):
                send_p[p * 2 + c, t] = tiles[t].astype(BF16)
        for side in range(2):
            p_copy(side, p).start()

    def ways(p):
        odd = lax.rem(p, 2)
        ahead = lax.rem(me + 3 + 2 * odd, 4)
        behind = lax.rem(me + 1 + 2 * odd, 4)
        return ahead, behind

    def far_copy(p):
        return remote(
            send_far.at[p], near_far.at[p], c_send.at[0, p], c_recv.at[0, p], ways(p)[0]
        )

    def next_copy(p):
        return remote(
            send_next.at[p], near_next.at[p], c_send.at[1, p], c_recv.at[1, p], ways(p)[0]
        )

    def back_copy(p):
        return remote(
            send_back.at[p], near_back.at[p], c_send.at[2, p], c_recv.at[2, p], ways(p)[1]
        )

    def forward(p):
        far_copy(p).wait_recv()
        for t in range(3):
            send_next[p, t] = (hold_next[p, t] + near_far[p, t].astype(F32)).astype(BF16)
        next_copy(p).start()

    def finish(p):
        next_copy(p).wait_recv()
        back_copy(p).wait_recv()
        for t in range(3):
            planes[t, pl.ds(p, PLANES, stride=PAIRS), :] = (
                hold_own[p, t] + near_next[p, t].astype(F32) + near_back[p, t].astype(F32)
            )

    @pl.loop(0, PAIRS)
    def _(p):
        for side in range(2):
            p_copy(side, p).wait_recv()
        for c in range(2):
            for side in range(2):
                tiles = [near_p[side, p * 2 + c, t] for t in range(3)]
                last = unpack_last(*[tile.astype(F32) for tile in tiles]).astype(BF16)
                tiles.append(last)
                for e in range(4):
                    lanes = slice((e % 2) * LANES, (e % 2 + 1) * LANES)
                    rim[c * 7 + 4 * side + e // 2, :, lanes] = tiles[e]
            for k in range(2):
                rim[c * 7 + 2 + k] = own_p[p * 4 + c * 2 + k]
            total = None
            for k in range(2):
                row = p * 4 + c * 2 + k
                stiff = apply(row, c * 7, 2 + k).astype(BF16)
                term = lax.dot_general(
                    rim[c * 7 + 2 + k], stiff, (((0,), (0,)), ((), ())),
                    preferred_element_type=F32,
                )
                total = term if total is None else total + term
            part[c] = total

        def share(col):
            start = pl.multiple_of((col // 2) * LANES + lax.rem(col, 2) * 48, 16)
            rows = pl.ds(start, 48)
            return pack4(
                part[0, rows, 0:LANES],
                part[0, rows, LANES : 2 * LANES],
                part[1, rows, 0:LANES],
                part[1, rows, LANES : 2 * LANES],
            )

        ahead, behind = ways(p)
        tiles = share(lax.rem(me + 2, 4))
        for t in range(3):
            send_far[p, t] = tiles[t].astype(BF16)
        far_copy(p).start()
        tiles = share(behind)
        for t in range(3):
            send_back[p, t] = tiles[t].astype(BF16)
        back_copy(p).start()
        tiles = share(ahead)
        for t in range(3):
            hold_next[p, t] = tiles[t]
        tiles = share(me)
        for t in range(3):
            hold_own[p, t] = tiles[t]

        @pl.when(p >= 1)
        def _():
            forward(p - 1)

        @pl.when(p >= 2)
        def _():
            finish(p - 2)

    forward(PAIRS - 1)
    finish(PAIRS - 2)
    finish(PAIRS - 1)

    @pl.loop(0, PLANES)
    def _(r):
        for t in range(3):
            rows = pl.ds(pl.multiple_of(r * PAIRS, PAIRS), PAIRS)
            out_ref[r, t] = planes[t, rows, :].astype(BF16)

    for side in range(2):
        label_copy(side).wait_send()

    @pl.loop(0, PAIRS)
    def _(p):
        for side in range(2):
            t_copy(side, p).wait_send()
            p_copy(side, p).wait_send()
        far_copy(p).wait_send()
        next_copy(p).wait_send()
        back_copy(p).wait_send()


def galerkin(slots, labels, off, diag, inv, tent):
    dma = pltpu.SemaphoreType.DMA
    hbm = pl.BlockSpec(memory_space=pl.ANY)
    return pl.pallas_call(
        galerkin_kernel,
        out_shape=jax.ShapeDtypeStruct((PLANES, 3, PAIRS, LANES), BF16),
        in_specs=[
            pl.BlockSpec(memory_space=pltpu.SMEM),
            pl.BlockSpec(memory_space=pltpu.VMEM),
            hbm,
            hbm,
            hbm,
            hbm,
        ],
        out_specs=pl.BlockSpec(memory_space=pltpu.VMEM),
        scratch_shapes=[
            pltpu.VMEM((ROWS, 4, B, B), BF16),
            pltpu.VMEM((ROWS, B, B), BF16),
            pltpu.VMEM((ROWS, B, B), BF16),
            pltpu.VMEM((ROWS, B, B), BF16),
            pltpu.VMEM((ROWS, B, LANES), BF16),
            pltpu.VMEM((ROWS, LANES), F32),
            pltpu.VMEM((2, ROWS, LANES), F32),
            pltpu.VMEM((PAIRS, 3, B, LANES), BF16),
            pltpu.VMEM((2, PAIRS, 3, B, LANES), BF16),
            pltpu.VMEM((ROWS, B, 2 * LANES), BF16),
            pltpu.VMEM((2 * PAIRS, 3, B, LANES), BF16),
            pltpu.VMEM((2, 2 * PAIRS, 3, B, LANES), BF16),
            pltpu.VMEM((14, B, 2 * LANES), BF16),
            pltpu.VMEM((2, 2 * LANES, 2 * LANES), F32),
            pltpu.VMEM((PAIRS, 3, 48, LANES), BF16),
            pltpu.VMEM((PAIRS, 3, 48, LANES), BF16),
            pltpu.VMEM((PAIRS, 3, 48, LANES), BF16),
            pltpu.VMEM((PAIRS, 3, 48, LANES), BF16),
            pltpu.VMEM((PAIRS, 3, 48, LANES), BF16),
            pltpu.VMEM((PAIRS, 3, 48, LANES), BF16),
            pltpu.VMEM((PAIRS, 3, 48, LANES), F32),
            pltpu.VMEM((PAIRS, 3, 48, LANES), F32),
            pltpu.VMEM((3, PLANES * PAIRS, LANES), F32),
            dma((3, PAIRS)),
            dma,
            dma((2,)),
            dma((2,)),
            dma((2, PAIRS)),
            dma((2, PAIRS)),
            dma((2, PAIRS)),
            dma((2, PAIRS)),
            dma((3, PAIRS)),
            dma((3, PAIRS)),
        ],
        compiler_params=pltpu.CompilerParams(
            collective_id=0, has_side_effects=True, vmem_limit_bytes=52 * 1024 * 1024
        ),
    )(slots, labels, off, diag, inv, tent)


def plane_device(r):
    z = r // 6
    return z * 8 + lax.rem(lax.rem(r, 6) + 2 * z + 2, 8)


def owner_kernel(planes_ref, target_ref, out_ref, gathered, sums, send, landed, wide, sems):
    me = lax.axis_index("row")
    z = me // 8
    place = lax.rem(lax.rem(me, 8) + 32 - 2 * z - 2, 8)
    holds = place < 6
    plane = z * 6 + place

    def plane_copy(r, target):
        return pltpu.make_async_remote_copy(
            src_ref=planes_ref.at[r],
            dst_ref=gathered.at[me],
            send_sem=sems.at[0],
            recv_sem=sems.at[1],
            device_id={"row": target},
            device_id_type=MESH,
        )

    def group_copy(target):
        return pltpu.make_async_remote_copy(
            src_ref=send.at[target],
            dst_ref=landed.at[plane],
            send_sem=sems.at[2],
            recv_sem=sems.at[3],
            device_id={"row": target},
            device_id_type=MESH,
        )

    barrier = pltpu.get_barrier_semaphore()

    @pl.loop(1, PEERS)
    def _(d):
        pl.semaphore_signal(
            barrier, inc=1, device_id={"row": lax.rem(me + d, PEERS)}, device_id_type=MESH
        )

    pl.semaphore_wait(barrier, PEERS - 1)

    @pl.loop(0, PLANES)
    def _(d):
        r = lax.rem(z * 6 + d, PLANES)
        target = plane_device(r)

        @pl.when(target != me)
        def _():
            plane_copy(r, target).start()

        @pl.when(target == me)
        def _():
            pltpu.make_async_copy(planes_ref.at[r], gathered.at[me], sems.at[1]).start()

    @pl.when(holds)
    def _():
        pltpu.make_async_copy(gathered, gathered, sems.at[1]).wait()
        tiles = [
            gathered[:, t].astype(F32).reshape(PEERS * PAIRS, LANES) for t in range(3)
        ]
        tiles.append(unpack_last(*tiles))
        tiles = [tile.astype(BF16) for tile in tiles]
        group = lax.broadcasted_iota(jnp.int32, (8 * PEERS, PEERS * PAIRS), 0)
        first = jnp.where(group == target_ref[0:1, :], 1.0, 0.0).astype(BF16)
        second = jnp.where(group == target_ref[1:2, :], 1.0, 0.0).astype(BF16)
        for c in range(2):
            total = dot(first, tiles[c]) + dot(second, tiles[2 + c])
            sums[:, c * 8 : (c + 1) * 8, :] = total.reshape(PEERS, 8, LANES)
        send[...] = sums[...].astype(BF16)

        @pl.loop(0, PEERS)
        def _(d):
            target = lax.rem(me + d, PEERS)

            @pl.when(target != me)
            def _():
                group_copy(target).start()

            @pl.when(target == me)
            def _():
                pltpu.make_async_copy(send.at[me], landed.at[plane], sems.at[3]).start()

    pltpu.make_async_copy(landed, landed, sems.at[3]).wait()
    wide[...] = landed[...].astype(F32).reshape(PLANES * 16, LANES)
    for g in range(8):
        first = wide[pl.ds(g, PLANES, stride=16), :]
        second = pltpu.roll(wide[pl.ds(8 + g, PLANES, stride=16), :], 96, 1)
        high = lax.broadcasted_iota(jnp.int32, first.shape, 1) >= B
        out_ref[g, :, 0:LANES] = jnp.where(high, second, first)
        out_ref[g, :, LANES : 2 * B] = second[:, 0 : 2 * B - LANES]

    @pl.loop(0, PLANES)
    def _(r):
        target = plane_device(r)

        @pl.when(target != me)
        def _():
            plane_copy(r, target).wait_send()

    @pl.when(holds)
    def _():
        @pl.loop(1, PEERS)
        def _(d):
            group_copy(lax.rem(me + d, PEERS)).wait_send()


def to_owners(planes, targets):
    vmem = pl.BlockSpec(memory_space=pltpu.VMEM)
    return pl.pallas_call(
        owner_kernel,
        out_shape=jax.ShapeDtypeStruct((8, PLANES, 2 * B), F32),
        in_specs=[vmem, vmem],
        out_specs=vmem,
        scratch_shapes=[
            pltpu.VMEM((PEERS, 3, PAIRS, LANES), BF16),
            pltpu.VMEM((PEERS, 16, LANES), F32),
            pltpu.VMEM((PEERS, 16, LANES), BF16),
            pltpu.VMEM((PLANES, 16, LANES), BF16),
            pltpu.VMEM((PLANES * 16, LANES), F32),
            pltpu.SemaphoreType.DMA((4,)),
        ],
        compiler_params=pltpu.CompilerParams(
            collective_id=1, has_side_effects=True, vmem_limit_bytes=32 * 1024 * 1024
        ),
    )(planes, targets)


def on_device(
    off_blocks,
    neighbour,
    active,
    diag_blocks,
    diag_inverse,
    tentative,
    aggregate,
    owner_row,
    owner_group,
):
    target = owner_row[:, 0] * 8 + owner_group
    targets = lax.all_gather(target, "row")
    targets = targets.reshape(PEERS * PAIRS, 2).T
    slots = jnp.where(active != 0, neighbour, 6).reshape(-1)
    labels = jnp.broadcast_to(aggregate.astype(F32)[:, None], (ROWS, LANES))
    planes = galerkin(slots, labels, off_blocks, diag_blocks, diag_inverse, tentative)
    return to_owners(planes, targets)


def solution(mesh):
    return jax.shard_map(
        on_device,
        mesh=mesh,
        in_specs=(
            P(("row", "col"), None, None, None),
            P(("row", "col"), None),
            P(("row", "col"), None),
            P(("row", "col"), None, None),
            P(("row", "col"), None, None),
            P(("row", "col"), None, None),
            P(("row", "col")),
            P("row", None),
            P("row"),
        ),
        out_specs=P("row", "col", None),
        check_vma=False,
    )
```

time: 510 us -> 188 us (0.37); the launches traced: 504 us -> 188 us
  waiting for transfers between devices: 321 us -> 0 us
  Pallas kernels: 0 us -> 161 us
  matrix products: 64.9 us -> 0 us
  local copies, waits for them, and re-layouts: 54.2 us -> 2.94 us
  starting transfers between devices: 33 us -> 0 us
  blocking collectives: 0 us -> 20.7 us
  other arithmetic: 17.3 us -> 2.12 us
  between operations: 13.7 us -> 0.69 us
    pallas_call x0 -> x2, Pallas kernels: none -> 161 us  [the longest x1 117 us: galerkin(): pl.pallas_call(galerkin_kernel, out_shape=jax.ShapeDtypeStruct((PLANES, 3...]
    all_to_all x2 -> x0, waiting for transfers between devices: 138 us -> none  [the longest x1 138 us: on_device(): lax.all_to_all(outgoing, 'row', split_axis=0, concat_axis=0, tiled=True)]
    ppermute x4 -> x0, waiting for transfers between devices: 128 us -> none  [the longest x2 126 us: with_halo(): lax.ppermute(lax.slice_in_dim(block, block.shape[dim] - width, None, axis...]
    dot_general x7 -> x0, matrix products: 64.9 us -> none  [the longest x2 24.5 us: apply_rows(): jnp.einsum('rsij,rsjw->riw', weights, near_rows, preferred_element_type=j...]
    reduce_scatter x1 -> x0, waiting for transfers between devices: 55.1 us -> none  [on_device(): lax.psum_scatter(partial_value, 'col', scatter_dimension=1, tiled=True)]
    gather x2 -> x0, local copies, waits for them, and re-layouts: 28.5 us -> none  [apply_rows(): near_rows = jnp.take(with_rim, near_index, axis=0)]
    all_to_all x2 -> x0, starting transfers between devices: 26 us -> none  [the longest x1 14.8 us: on_device(): lax.all_to_all(slot_groups, 'row', split_axis=0, concat_axis=0, tiled=True)]
    unnamed x0 -> x1, blocking collectives: none -> 20.7 us
  transfers between devices with their start and end apart: 7 -> 0, of which waited for: 6 -> 0; matrix products, arithmetic and copies ran while one was open for 6% -> 0% of each run, Pallas kernels for 0% -> 0%
where the time goes in v1:
time: 188 us
  Pallas kernels  161 us (86%)
  blocking collectives  20.7 us (11%)
  local copies, waits for them, and re-layouts  2.94 us (2%)
  other arithmetic  2.12 us (1%)
    pallas_call x1, Pallas kernels, galerkin(): pl.pallas_call(galerkin_kernel, out_shape=jax.ShapeDtypeStruct((PLANES, 3...  117 us
    pallas_call x1, Pallas kernels, to_owners(): pl.pallas_call(owner_kernel, out_shape=jax.ShapeDtypeStruct((8, PLANES, 2...  44.3 us
    unnamed x1, blocking collectives  20.7 us

profile of v1, /device:TPU:1, one launch (start us, length us, event | category | flops | bytes accessed | tf_op | source)
XLA Modules:
  0.0 187.8 jit_solution(3436186821722055906)
XLA Ops:
  0.0 1.3 dynamic-slice
  1.9 0.7 convert_element_type.3
  2.6 0.7 compare_select_fusion
  3.3 0.8 fusion
  4.0 20.7 %all-reduce = s32[2048]{0:T(1024)S(1)} all-reduce(s32[2048]{0:T(1024)S(1)} %fusion), channel_id=2, replica_groups=mesh['row'=64,'col'=4] {'row'}, use_global_device_ids=true, to_apply=%add | all-reduce | flops 2048 | bytes 16384
  24.8 0.1 copy.10
  24.9 0.1 reshape.9.slot_ref
  25.0 0.1 broadcast_in_dim.11.label_ref
  25.1 0.5 reshape.10
  25.5 0.2 copy.11
  25.7 117.0 %shard_map.91.planes_ref = bf16[48,3,16,128]{3,2,1,0:T(8,128)(2,1)S(1)} custom-call(s32[256]{0:T(256)S(1)} %reshape.9.slot_ref, f32[64,128]{1,0:T(8,128)S(1)} %broadcast_in_dim.11.label_ref, bf16[64,4,96,96]{3,2,1,0:T(8,128)(2,1)} %off_hbm.1, bf16[64,96,96]{2,1,0:T(8,128)(2,1)} %diag_hbm.1, bf16[64,96,96]{2,1,0:T(8,128)(2,1)} %inv_hbm.1, ...), custom_call_target="tpu_custom_call" | custom-call | tf_op jit(solution)/shard_map/pallas_call | solution.py:319
  142.8 44.3 %shard_map.92 = f32[8,48,192]{2,1,0:T(8,128)S(1)} custom-call(bf16[48,3,16,128]{3,2,1,0:T(8,128)(2,1)S(1)} %shard_map.91.planes_ref, s32[2,1024]{1,0:T(2,128)S(1)} %bitcast.6), custom_call_target="tpu_custom_call" | custom-call | tf_op jit(solution)/shard_map/pallas_call | solution.py:481
  187.0 0.7 copy.14
  (1 shorter events, 0.0 us)

commit v2 on v1

v2 whole, which is shorter than its diff:
```python
import jax
import jax.numpy as jnp
from jax import lax
from jax.experimental import pallas as pl
from jax.experimental.pallas import tpu as pltpu
from jax.sharding import PartitionSpec as P

MESH = pl.DeviceIdType.MESH
F32 = jnp.float32
BF16 = jnp.bfloat16
B = 96
LANES = 128
OMEGA = 0.6
ROWS = 64
PAIRS = 16
PEERS = 64
PLANES = 48
CHUNKS = 4
WINDOW = 3
LAG = 3


def pack4(b0, b1, b2, b3):
    high = lax.broadcasted_iota(jnp.int32, b0.shape, 1) >= B
    return (
        jnp.where(high, pltpu.roll(b3, 96, 1), b0),
        jnp.where(high, pltpu.roll(b3, 64, 1), b1),
        jnp.where(high, pltpu.roll(b3, 32, 1), b2),
    )


def unpack_last(t0, t1, t2):
    lane = lax.broadcasted_iota(jnp.int32, t0.shape, 1)
    return jnp.where(
        lane < 32,
        pltpu.roll(t0, 32, 1),
        jnp.where(lane < 64, pltpu.roll(t1, 64, 1), pltpu.roll(t2, 96, 1)),
    )


def dot(a, b):
    return lax.dot_general(a, b, (((1,), (0,)), ((), ())), preferred_element_type=F32)


def plane_device(r):
    z = r // 6
    return z * 8 + lax.rem(lax.rem(r, 6) + 2 * z + 2, 8)


def galerkin_kernel(
    near_smem,
    active_smem,
    label_smem,
    owner_smem,
    group_smem,
    off_hbm,
    diag_hbm,
    inv_hbm,
    tent_hbm,
    out_ref,
    off,
    diag,
    inv,
    tent,
    wide,
    send_label,
    near_label,
    send_t,
    near_t,
    own_p,
    send_p,
    near_p,
    rim,
    part,
    send_far,
    send_next,
    send_back,
    near_far,
    near_next,
    near_back,
    hold_next,
    hold_own,
    staging,
    send_target,
    near_target,
    onehot,
    send_plane,
    near_plane,
    total_sum,
    send_group,
    near_group,
    final,
    load_sem,
    tent_sem,
    label_send,
    label_recv,
    t_send,
    t_recv,
    p_send,
    p_recv,
    c_send,
    c_recv,
    target_sem,
    plane_send,
    plane_recv,
    group_sem,
):
    me = lax.axis_index("col")
    right, left = lax.rem(me + 1, 4), lax.rem(me + 3, 4)
    tile = lax.axis_index("row")
    z = tile // 8
    place = lax.rem(lax.rem(tile, 8) + 32 - 2 * z - 2, 8)
    holds = place < 6
    plane = z * 6 + place

    def loads(p):
        rows = pl.ds(p * 4, 4)
        return [
            pltpu.make_async_copy(off_hbm.at[rows], off.at[rows], load_sem.at[0, p]),
            pltpu.make_async_copy(diag_hbm.at[rows], diag.at[rows], load_sem.at[1, p]),
            pltpu.make_async_copy(inv_hbm.at[rows], inv.at[rows], load_sem.at[2, p]),
        ]

    def remote(src, dst, send_sem, recv_sem, col):
        return pltpu.make_async_remote_copy(
            src_ref=src,
            dst_ref=dst,
            send_sem=send_sem,
            recv_sem=recv_sem,
            device_id={"col": col},
            device_id_type=MESH,
        )

    def along_row(src, dst, send_sem, recv_sem, target):
        return pltpu.make_async_remote_copy(
            src_ref=src,
            dst_ref=dst,
            send_sem=send_sem,
            recv_sem=recv_sem,
            device_id={"row": target},
            device_id_type=MESH,
        )

    tent_copy = pltpu.make_async_copy(tent_hbm, tent, tent_sem)
    tent_copy.start()

    barrier = pltpu.get_barrier_semaphore()
    for peer in (left, right):
        pl.semaphore_signal(barrier, inc=1, device_id={"col": peer}, device_id_type=MESH)

    @pl.loop(1, PEERS)
    def _(d):
        pl.semaphore_signal(
            barrier, inc=1, device_id={"row": lax.rem(tile + d, PEERS)}, device_id_type=MESH
        )

    @pl.loop(0, PAIRS)
    def _(p):
        for copy in loads(p):
            copy.start()

    rim[6] = jnp.zeros_like(rim[6])
    rim[13] = jnp.zeros_like(rim[13])

    @pl.loop(0, ROWS)
    def _(f):
        send_label[pl.ds(f, 1), :] = jnp.full((1, LANES), label_smem[f], jnp.int32).astype(F32)

    sub = lax.broadcasted_iota(jnp.int32, (8, LANES), 0)
    lane = lax.broadcasted_iota(jnp.int32, (8, LANES), 1)
    mine = jnp.zeros((8, LANES), jnp.int32)
    for q in range(32):
        here = (sub == q // 8) & (lane == lax.rem(tile, 16) * 8 + q % 8)
        mine = jnp.where(here, owner_smem[q] * 8 + group_smem[q], mine)
    send_target[...] = mine

    tent_copy.wait()

    @pl.loop(0, PAIRS)
    def _(p):
        for e in range(4):
            wide[p * 4 + e, :, 0:B] = tent[p * 4 + e]
        tiles = pack4(*[wide[p * 4 + e].astype(F32) for e in range(4)])
        for t in range(3):
            send_t[p, t] = tiles[t].astype(BF16)

    pl.semaphore_wait(barrier, PEERS + 1)

    def label_copy(side):
        return remote(
            send_label, near_label.at[side], label_send.at[side], label_recv.at[side],
            right if side == 0 else left,
        )

    def t_copy(side, p):
        return remote(
            send_t.at[p], near_t.at[side, p], t_send.at[side, p], t_recv.at[side, p],
            right if side == 0 else left,
        )

    def p_copy(side, p):
        rows = pl.ds(p * 2, 2)
        return remote(
            send_p.at[rows], near_p.at[side, rows], p_send.at[side, p], p_recv.at[side, p],
            right if side == 0 else left,
        )

    def target_copy(target):
        return along_row(
            send_target, near_target.at[tile], target_sem.at[0], target_sem.at[1], target
        )

    for side in range(2):
        label_copy(side).start()

    @pl.loop(0, PAIRS)
    def _(p):
        for side in range(2):
            t_copy(side, p).start()

    @pl.loop(0, PLANES)
    def _(r):
        target = plane_device(r)

        @pl.when(target != tile)
        def _():
            target_copy(target).start()

    @pl.when(holds)
    def _():
        pltpu.make_async_copy(send_target, near_target.at[tile], target_sem.at[1]).start()

    for side in range(2):
        label_copy(side).wait_recv()

    def apply(row, near_base, own):
        total = dot(diag[row], rim[near_base + own])
        for s in range(4):
            on = active_smem[s, row]
            slot = near_smem[s, row] * on + 6 * (1 - on)
            total = total + dot(off[row, s], rim[near_base + slot])
        return total

    @pl.loop(0, PAIRS)
    def _(p):
        for side in range(2):
            t_copy(side, p).wait_recv()
        for copy in loads(p):
            copy.wait()

        def spread(e, position, block, label):
            zero = jnp.zeros_like(block)
            at = (e // 2) * 7 + position + e % 2
            rim[at, :, 0:LANES] = jnp.where(label == 0.0, block, zero).astype(BF16)
            rim[at, :, LANES : 2 * LANES] = jnp.where(label == 1.0, block, zero).astype(BF16)

        for side in range(2):
            tiles = [near_t[side, p, t].astype(F32) for t in range(3)]
            tiles.append(unpack_last(*tiles))
            for e in range(4):
                spread(e, 4 * side, tiles[e], near_label[side, pl.ds(p * 4 + e, 1), :])
        for e in range(4):
            spread(e, 2, wide[p * 4 + e].astype(F32), send_label[pl.ds(p * 4 + e, 1), :])

        for c in range(2):
            blocks = []
            for k in range(2):
                row = p * 4 + c * 2 + k
                smooth = apply(row, c * 7, 2 + k).astype(BF16)
                prolong = rim[c * 7 + 2 + k].astype(F32) - OMEGA * dot(inv[row], smooth)
                rounded = prolong.astype(BF16)
                own_p[row] = rounded
                back = rounded.astype(F32)
                blocks += [back[:, 0:LANES], back[:, LANES : 2 * LANES]]
            tiles = pack4(*blocks)
            for t in range(3):
                send_p[p * 2 + c, t] = tiles[t].astype(BF16)

        @pl.when(p < WINDOW)
        def _():
            for side in range(2):
                p_copy(side, p).start()

    @pl.when(holds)
    def _():
        pltpu.make_async_copy(near_target, near_target, target_sem.at[1]).wait()
        group = lax.broadcasted_iota(jnp.int32, (8 * PEERS, LANES), 0)
        for k in range(4):
            named = near_target[16 * k]
            for t in range(1, 16):
                named = named + near_target[16 * k + t]
            for ch in range(CHUNKS):
                onehot[ch, :, k * LANES : (k + 1) * LANES] = jnp.where(
                    group == named[ch : ch + 1, :], 1.0, 0.0
                ).astype(BF16)

    def ways(p):
        odd = lax.rem(p, 2)
        ahead = lax.rem(me + 3 + 2 * odd, 4)
        behind = lax.rem(me + 1 + 2 * odd, 4)
        return ahead, behind

    def far_copy(p):
        return remote(
            send_far.at[p], near_far.at[p], c_send.at[0, p], c_recv.at[0, p], ways(p)[0]
        )

    def next_copy(p):
        return remote(
            send_next.at[p], near_next.at[p], c_send.at[1, p], c_recv.at[1, p], ways(p)[0]
        )

    def back_copy(p):
        return remote(
            send_back.at[p], near_back.at[p], c_send.at[2, p], c_recv.at[2, p], ways(p)[1]
        )

    def plane_copy(ch, r, target):
        return along_row(
            send_plane.at[ch, r], near_plane.at[ch, tile], plane_send.at[ch], plane_recv.at[ch],
            target,
        )

    def forward(p):
        far_copy(p).wait_recv()
        for t in range(3):
            send_next[p, t] = (hold_next[p, t] + near_far[p, t].astype(F32)).astype(BF16)
        next_copy(p).start()

    def finish(p):
        next_copy(p).wait_recv()
        back_copy(p).wait_recv()
        tiles = [
            hold_own[p, t] + near_next[p, t].astype(F32) + near_back[p, t].astype(F32)
            for t in range(3)
        ]
        tiles.append(unpack_last(*tiles))
        for e in range(4):
            at = (e % 2) * 8 + lax.rem(p, 4) * 2 + e // 2
            staging[pl.ds(at, PLANES, stride=16), :] = tiles[e]

        @pl.when(lax.rem(p, 4) == 3)
        def _():
            ch = p // 4

            @pl.loop(0, PLANES)
            def _(d):
                r = lax.rem(z * 6 + d, PLANES)
                target = plane_device(r)
                rows = pl.ds(pl.multiple_of(r * 16, 16), 16)
                send_plane[ch, r] = staging[rows, :].astype(BF16)

                @pl.when(target != tile)
                def _():
                    plane_copy(ch, r, target).start()

                @pl.when(target == tile)
                def _():
                    pltpu.make_async_copy(
                        send_plane.at[ch, r], near_plane.at[ch, tile], plane_recv.at[ch]
                    ).start()

    @pl.loop(0, PAIRS)
    def _(p):
        for side in range(2):
            p_copy(side, p).wait_recv()
        for c in range(2):
            for side in range(2):
                tiles = [near_p[side, p * 2 + c, t] for t in range(3)]
                last = unpack_last(*[tile.astype(F32) for tile in tiles]).astype(BF16)
                tiles.append(last)
                for e in range(4):
                    lanes = slice((e % 2) * LANES, (e % 2 + 1) * LANES)
                    rim[c * 7 + 4 * side + e // 2, :, lanes] = tiles[e]
            for k in range(2):
                rim[c * 7 + 2 + k] = own_p[p * 4 + c * 2 + k]
            total = None
            for k in range(2):
                row = p * 4 + c * 2 + k
                stiff = apply(row, c * 7, 2 + k).astype(BF16)
                term = lax.dot_general(
                    rim[c * 7 + 2 + k], stiff, (((0,), (0,)), ((), ())),
                    preferred_element_type=F32,
                )
                total = term if total is None else total + term
            part[c] = total

        def share(col):
            start = pl.multiple_of((col // 2) * LANES + lax.rem(col, 2) * 48, 16)
            rows = pl.ds(start, 48)
            return pack4(
                part[0, rows, 0:LANES],
                part[0, rows, LANES : 2 * LANES],
                part[1, rows, 0:LANES],
                part[1, rows, LANES : 2 * LANES],
            )

        ahead, behind = ways(p)
        tiles = share(lax.rem(me + 2, 4))
        for t in range(3):
            send_far[p, t] = tiles[t].astype(BF16)
        far_copy(p).start()
        tiles = share(behind)
        for t in range(3):
            send_back[p, t] = tiles[t].astype(BF16)
        back_copy(p).start()

        @pl.when(p + WINDOW < PAIRS)
        def _():
            for side in range(2):
                p_copy(side, p + WINDOW).start()

        tiles = share(ahead)
        for t in range(3):
            hold_next[p, t] = tiles[t]
        tiles = share(me)
        for t in range(3):
            hold_own[p, t] = tiles[t]

        @pl.when(p >= LAG)
        def _():
            forward(p - LAG)

        @pl.when(p >= 2 * LAG)
        def _():
            finish(p - 2 * LAG)

    @pl.loop(PAIRS - LAG, PAIRS)
    def _(p):
        forward(p)

    @pl.loop(PAIRS - 2 * LAG, PAIRS)
    def _(p):
        finish(p)

    def group_copy(target):
        return along_row(
            send_group.at[target], near_group.at[plane], group_sem.at[0], group_sem.at[1], target
        )

    @pl.when(holds)
    def _():
        for ch in range(CHUNKS):
            here = near_plane.at[ch]
            pltpu.make_async_copy(here, here, plane_recv.at[ch]).wait()
            rows = near_plane[ch].astype(F32)
            both = [rows[:, c * 8 : c * 8 + 8, :].reshape(8 * PEERS, LANES) for c in range(2)]
            block = jnp.concatenate(both, axis=1).astype(BF16)
            term = dot(onehot[ch], block)
            total_sum[...] = term if ch == 0 else total_sum[...] + term
        both = [
            total_sum[:, c * LANES : (c + 1) * LANES].reshape(PEERS, 8, LANES) for c in range(2)
        ]
        send_group[...] = jnp.concatenate(both, axis=1).astype(BF16)

        @pl.loop(0, PEERS)
        def _(d):
            target = lax.rem(tile + d, PEERS)

            @pl.when(target != tile)
            def _():
                group_copy(target).start()

            @pl.when(target == tile)
            def _():
                pltpu.make_async_copy(
                    send_group.at[tile], near_group.at[plane], group_sem.at[1]
                ).start()

    pltpu.make_async_copy(near_group, near_group, group_sem.at[1]).wait()
    final[...] = near_group[...].astype(F32).reshape(PLANES * 16, LANES)
    for g in range(8):
        first = final[pl.ds(g, PLANES, stride=16), :]
        second = pltpu.roll(final[pl.ds(8 + g, PLANES, stride=16), :], 96, 1)
        high = lax.broadcasted_iota(jnp.int32, first.shape, 1) >= B
        out_ref[g, :, 0:LANES] = jnp.where(high, second, first)
        out_ref[g, :, LANES : 2 * B] = second[:, 0 : 2 * B - LANES]

    for side in range(2):
        label_copy(side).wait_send()

    @pl.loop(0, PAIRS)
    def _(p):
        for side in range(2):
            t_copy(side, p).wait_send()
            p_copy(side, p).wait_send()
        far_copy(p).wait_send()
        next_copy(p).wait_send()
        back_copy(p).wait_send()

    @pl.loop(0, PLANES)
    def _(r):
        target = plane_device(r)

        @pl.when(target != tile)
        def _():
            target_copy(target).wait_send()
            for ch in range(CHUNKS):
                plane_copy(ch, r, target).wait_send()

    @pl.when(holds)
    def _():
        @pl.loop(1, PEERS)
        def _(d):
            group_copy(lax.rem(tile + d, PEERS)).wait_send()


def galerkin(*operands):
    dma = pltpu.SemaphoreType.DMA
    hbm = pl.BlockSpec(memory_space=pl.ANY)
    scalars = pl.BlockSpec(memory_space=pltpu.SMEM)
    share = (PAIRS, 3, 48, LANES)
    return pl.pallas_call(
        galerkin_kernel,
        out_shape=jax.ShapeDtypeStruct((8, PLANES, 2 * B), F32),
        in_specs=[scalars] * 5 + [hbm] * 4,
        out_specs=pl.BlockSpec(memory_space=pltpu.VMEM),
        scratch_shapes=[
            pltpu.VMEM((ROWS, 4, B, B), BF16),
            pltpu.VMEM((ROWS, B, B), BF16),
            pltpu.VMEM((ROWS, B, B), BF16),
            pltpu.VMEM((ROWS, B, B), BF16),
            pltpu.VMEM((ROWS, B, LANES), BF16),
            pltpu.VMEM((ROWS, LANES), F32),
            pltpu.VMEM((2, ROWS, LANES), F32),
            pltpu.VMEM((PAIRS, 3, B, LANES), BF16),
            pltpu.VMEM((2, PAIRS, 3, B, LANES), BF16),
            pltpu.VMEM((ROWS, B, 2 * LANES), BF16),
            pltpu.VMEM((2 * PAIRS, 3, B, LANES), BF16),
            pltpu.VMEM((2, 2 * PAIRS, 3, B, LANES), BF16),
            pltpu.VMEM((14, B, 2 * LANES), BF16),
            pltpu.VMEM((2, 2 * LANES, 2 * LANES), F32),
            pltpu.VMEM(share, BF16),
            pltpu.VMEM(share, BF16),
            pltpu.VMEM(share, BF16),
            pltpu.VMEM(share, BF16),
            pltpu.VMEM(share, BF16),
            pltpu.VMEM(share, BF16),
            pltpu.VMEM(share, F32),
            pltpu.VMEM(share, F32),
            pltpu.VMEM((PLANES * 16, LANES), F32),
            pltpu.VMEM((8, LANES), jnp.int32),
            pltpu.VMEM((PEERS, 8, LANES), jnp.int32),
            pltpu.VMEM((CHUNKS, 8 * PEERS, 4 * LANES), BF16),
            pltpu.VMEM((CHUNKS, PLANES, 16, LANES), BF16),
            pltpu.VMEM((CHUNKS, PEERS, 16, LANES), BF16),
            pltpu.VMEM((8 * PEERS, 2 * LANES), F32),
            pltpu.VMEM((PEERS, 16, LANES), BF16),
            pltpu.VMEM((PLANES, 16, LANES), BF16),
            pltpu.VMEM((PLANES * 16, LANES), F32),
            dma((3, PAIRS)),
            dma,
            dma((2,)),
            dma((2,)),
            dma((2, PAIRS)),
            dma((2, PAIRS)),
            dma((2, PAIRS)),
            dma((2, PAIRS)),
            dma((3, PAIRS)),
            dma((3, PAIRS)),
            dma((2,)),
            dma((CHUNKS,)),
            dma((CHUNKS,)),
            dma((2,)),
        ],
        compiler_params=pltpu.CompilerParams(
            collective_id=0, has_side_effects=True, vmem_limit_bytes=52 * 1024 * 1024
        ),
    )(*operands)


def on_device(
    off_blocks,
    neighbour,
    active,
    diag_blocks,
    diag_inverse,
    tentative,
    aggregate,
    owner_row,
    owner_group,
):
    return galerkin(
        neighbour.T,
        active.T,
        aggregate,
        owner_row[:, 0],
        owner_group,
        off_blocks,
        diag_blocks,
        diag_inverse,
        tentative,
    )


def solution(mesh):
    return jax.shard_map(
        on_device,
        mesh=mesh,
        in_specs=(
            P(("row", "col"), None, None, None),
            P(("row", "col"), None),
            P(("row", "col"), None),
            P(("row", "col"), None, None),
            P(("row", "col"), None, None),
            P(("row", "col"), None, None),
            P(("row", "col")),
            P("row", None),
            P("row"),
        ),
        out_specs=P("row", "col", None),
        check_vma=False,
    )
```

time: 188 us -> 142 us (0.76)
  Pallas kernels: 161 us -> 137 us
  blocking collectives: 20.7 us -> 0 us
  local copies, waits for them, and re-layouts: 2.94 us -> 5.48 us
  other arithmetic: 2.12 us -> 0 us
    pallas_call x2 -> x1, Pallas kernels: 161 us -> 137 us  [galerkin(): pl.pallas_call(galerkin_kernel, out_shape=jax.ShapeDtypeStruct((8, PLANES...]
    unnamed x1 -> x0, blocking collectives: 20.7 us -> none
    unnamed x3 -> x13, local copies, waits for them, and re-layouts: 2.01 us -> 5.48 us
where the time goes in v2:
time: 142 us
  Pallas kernels  137 us (96%)
  local copies, waits for them, and re-layouts  5.48 us (4%)
    pallas_call x1, Pallas kernels, galerkin(): pl.pallas_call(galerkin_kernel, out_shape=jax.ShapeDtypeStruct((8, PLANES...  137 us
    unnamed x13, local copies, waits for them, and re-layouts  5.48 us

profile of v2, /device:TPU:1, one launch (start us, length us, event | category | flops | bytes accessed | tf_op | source)
XLA Modules:
  0.0 142.3 jit_solution(3752657140012805941)
XLA Ops:
  0.0 0.0 copy-start
  0.0 1.4 copy-done
  1.4 0.0 copy-start.1
  1.4 0.7 copy-done.1
  2.1 0.0 copy-start.2
  2.1 0.7 copy-done.2
  2.8 0.0 copy-start.3
  2.8 0.7 copy-done.3
  3.4 0.0 copy-start.4
  3.4 0.7 copy-done.4
  4.1 0.0 copy-start.5
  4.1 0.7 copy-done.5
  4.7 136.8 %shard_map.91 = f32[8,48,192]{2,1,0:T(8,128)S(1)} custom-call(s32[4,64]{1,0:T(4,128)S(1)} %bitcast.3, s32[4,64]{1,0:T(4,128)S(1)} %bitcast.4, s32[64]{0:T(128)S(1)} %copy-done.3, s32[32]{0:T(128)S(1)} %bitcast.5, s32[32]{0:T(128)S(1)} %copy-done.5, bf16[64,4,96,96]{3,2,1,0:T(8,128)(2,1)} %off_hbm.1, bf16[64,96,96]{2,1,0:T(8,128)(2,1)S(1)} %copy-done, ...), custom_call_target="tpu_custom_call" | custom-call | tf_op jit(solution)/shard_map/pallas_call | solution.py:513
  141.5 0.7 copy.11
Async XLA Ops:
  0.0 1.4 copy-start
  1.4 0.7 copy-start.1
  2.1 0.7 copy-start.2
  2.8 0.7 copy-start.3
  3.4 0.7 copy-start.4
  4.1 0.7 copy-start.5

commit v3 on v2

--- a/solution.py
+++ b/solution.py
@@ -18,6 +18,8 @@
 CHUNKS = 4
 WINDOW = 3
 LAG = 3
+EARLY = 4
+BITS = 6
 
 
 def pack4(b0, b1, b2, b3):
@@ -48,16 +50,21 @@
 
 
 def galerkin_kernel(
+    near_hbm,
+    active_hbm,
+    label_hbm,
+    owner_hbm,
+    group_hbm,
+    off_hbm,
+    diag_hbm,
+    inv_hbm,
+    tent_hbm,
+    out_ref,
     near_smem,
     active_smem,
     label_smem,
     owner_smem,
     group_smem,
-    off_hbm,
-    diag_hbm,
-    inv_hbm,
-    tent_hbm,
-    out_ref,
     off,
     diag,
     inv,
@@ -92,6 +99,8 @@
     final,
     load_sem,
     tent_sem,
+    small_sem,
+    round_sem,
     label_send,
     label_recv,
     t_send,
@@ -141,31 +150,112 @@
             device_id_type=MESH,
         )
 
-    tent_copy = pltpu.make_async_copy(tent_hbm, tent, tent_sem)
-    tent_copy.start()
+    def tent_load(p):
+        rows = pl.ds(p * 4, 4)
+        return pltpu.make_async_copy(tent_hbm.at[rows], tent.at[rows], tent_sem.at[p])
+
+    small = [
+        pltpu.make_async_copy(src, dst, small_sem.at[i])
+        for i, (src, dst) in enumerate(
+            [
+                (label_hbm, label_smem),
+                (near_hbm, near_smem),
+                (active_hbm, active_smem),
+                (owner_hbm, owner_smem),
+                (group_hbm, group_smem),
+            ]
+        )
+    ]
+
+    def partner(b):
+        size = 1 << b
+        return tile + size * (1 - 2 * lax.rem(tile // size, 2))
 
     barrier = pltpu.get_barrier_semaphore()
     for peer in (left, right):
         pl.semaphore_signal(barrier, inc=1, device_id={"col": peer}, device_id_type=MESH)
-
-    @pl.loop(1, PEERS)
-    def _(d):
-        pl.semaphore_signal(
-            barrier, inc=1, device_id={"row": lax.rem(tile + d, PEERS)}, device_id_type=MESH
-        )
+    for b in range(BITS):
+        pl.semaphore_signal(barrier, inc=1, device_id={"row": partner(b)}, device_id_type=MESH)
+
+    for copy in small:
+        copy.start()
 
     @pl.loop(0, PAIRS)
     def _(p):
-        for copy in loads(p):
-            copy.start()
-
-    rim[6] = jnp.zeros_like(rim[6])
-    rim[13] = jnp.zeros_like(rim[13])
+        tent_load(p).start()
+
+    small[0].wait()
 
     @pl.loop(0, ROWS)
     def _(f):
         send_label[pl.ds(f, 1), :] = jnp.full((1, LANES), label_smem[f], jnp.int32).astype(F32)
 
+    def pack_tent(p):
+        tent_load(p).wait()
+        for e in range(4):
+            wide[p * 4 + e, :, 0:B] = tent[p * 4 + e]
+        tiles = pack4(*[wide[p * 4 + e].astype(F32) for e in range(4)])
+        for t in range(3):
+            send_t[p, t] = tiles[t].astype(BF16)
+
+    @pl.loop(0, EARLY)
+    def _(p):
+        pack_tent(p)
+
+    pl.semaphore_wait(barrier, 2 + BITS)
+
+    def label_copy(side):
+        return remote(
+            send_label, near_label.at[side], label_send.at[side], label_recv.at[side],
+            right if side == 0 else left,
+        )
+
+    def t_copy(side, p):
+        return remote(
+            send_t.at[p], near_t.at[side, p], t_send.at[side, p], t_recv.at[side, p],
+            right if side == 0 else left,
+        )
+
+    def p_copy(side, p):
+        rows = pl.ds(p * 2, 2)
+        return remote(
+            send_p.at[rows], near_p.at[side, rows], p_send.at[side, p], p_recv.at[side, p],
+            right if side == 0 else left,
+        )
+
+    def target_copy(target):
+        return along_row(
+            send_target, near_target.at[tile], target_sem.at[0], target_sem.at[1], target
+        )
+
+    for side in range(2):
+        label_copy(side).start()
+
+    @pl.loop(0, PAIRS)
+    def _(p):
+        @pl.when(p >= EARLY)
+        def _():
+            pack_tent(p)
+
+        for side in range(2):
+            t_copy(side, p).start()
+
+    @pl.loop(0, PAIRS)
+    def _(p):
+        for copy in loads(p):
+            copy.start()
+
+    rim[6] = jnp.zeros_like(rim[6])
+    rim[13] = jnp.zeros_like(rim[13])
+
+    for b in range(BITS):
+        pl.semaphore_signal(
+            round_sem.at[b], inc=1, device_id={"row": partner(b)}, device_id_type=MESH
+        )
+        pl.semaphore_wait(round_sem.at[b], 1)
+
+    for copy in small[1:]:
+        copy.wait()
     sub = lax.broadcasted_iota(jnp.int32, (8, LANES), 0)
     lane = lax.broadcasted_iota(jnp.int32, (8, LANES), 1)
     mine = jnp.zeros((8, LANES), jnp.int32)
@@ -174,53 +264,9 @@
         mine = jnp.where(here, owner_smem[q] * 8 + group_smem[q], mine)
     send_target[...] = mine
 
-    tent_copy.wait()
-
-    @pl.loop(0, PAIRS)
-    def _(p):
-        for e in range(4):
-            wide[p * 4 + e, :, 0:B] = tent[p * 4 + e]
-        tiles = pack4(*[wide[p * 4 + e].astype(F32) for e in range(4)])
-        for t in range(3):
-            send_t[p, t] = tiles[t].astype(BF16)
-
-    pl.semaphore_wait(barrier, PEERS + 1)
-
-    def label_copy(side):
-        return remote(
-            send_label, near_label.at[side], label_send.at[side], label_recv.at[side],
-            right if side == 0 else left,
-        )
-
-    def t_copy(side, p):
-        return remote(
-            send_t.at[p], near_t.at[side, p], t_send.at[side, p], t_recv.at[side, p],
-            right if side == 0 else left,
-        )
-
-    def p_copy(side, p):
-        rows = pl.ds(p * 2, 2)
-        return remote(
-            send_p.at[rows], near_p.at[side, rows], p_send.at[side, p], p_recv.at[side, p],
-            right if side == 0 else left,
-        )
-
-    def target_copy(target):
-        return along_row(
-            send_target, near_target.at[tile], target_sem.at[0], target_sem.at[1], target
-        )
-
-    for side in range(2):
-        label_copy(side).start()
-
-    @pl.loop(0, PAIRS)
-    def _(p):
-        for side in range(2):
-            t_copy(side, p).start()
-
     @pl.loop(0, PLANES)
-    def _(r):
-        target = plane_device(r)
+    def _(d):
+        target = plane_device(lax.rem(tile + d, PLANES))
 
         @pl.when(target != tile)
         def _():
@@ -345,7 +391,7 @@
 
             @pl.loop(0, PLANES)
             def _(d):
-                r = lax.rem(z * 6 + d, PLANES)
+                r = lax.rem(tile + d, PLANES)
                 target = plane_device(r)
                 rows = pl.ds(pl.multiple_of(r * 16, 16), 16)
                 send_plane[ch, r] = staging[rows, :].astype(BF16)
@@ -467,6 +513,28 @@
                     send_group.at[tile], near_group.at[plane], group_sem.at[1]
                 ).start()
 
+    for side in range(2):
+        label_copy(side).wait_send()
+
+    @pl.loop(0, PAIRS)
+    def _(p):
+        for side in range(2):
+            t_copy(side, p).wait_send()
+            p_copy(side, p).wait_send()
+        far_copy(p).wait_send()
+        next_copy(p).wait_send()
+        back_copy(p).wait_send()
+
+    @pl.loop(0, PLANES)
+    def _(r):
+        target = plane_device(r)
+
+        @pl.when(target != tile)
+        def _():
+            target_copy(target).wait_send()
+            for ch in range(CHUNKS):
+                plane_copy(ch, r, target).wait_send()
+
     pltpu.make_async_copy(near_group, near_group, group_sem.at[1]).wait()
     final[...] = near_group[...].astype(F32).reshape(PLANES * 16, LANES)
     for g in range(8):
@@ -476,28 +544,6 @@
         out_ref[g, :, 0:LANES] = jnp.where(high, second, first)
         out_ref[g, :, LANES : 2 * B] = second[:, 0 : 2 * B - LANES]
 
-    for side in range(2):
-        label_copy(side).wait_send()
-
-    @pl.loop(0, PAIRS)
-    def _(p):
-        for side in range(2):
-            t_copy(side, p).wait_send()
-            p_copy(side, p).wait_send()
-        far_copy(p).wait_send()
-        next_copy(p).wait_send()
-        back_copy(p).wait_send()
-
-    @pl.loop(0, PLANES)
-    def _(r):
-        target = plane_device(r)
-
-        @pl.when(target != tile)
-        def _():
-            target_copy(target).wait_send()
-            for ch in range(CHUNKS):
-                plane_copy(ch, r, target).wait_send()
-
     @pl.when(holds)
     def _():
         @pl.loop(1, PEERS)
@@ -507,15 +553,19 @@
 
 def galerkin(*operands):
     dma = pltpu.SemaphoreType.DMA
-    hbm = pl.BlockSpec(memory_space=pl.ANY)
-    scalars = pl.BlockSpec(memory_space=pltpu.SMEM)
+    hbm = pl.BlockSpec(memory_space=pltpu.HBM)
     share = (PAIRS, 3, 48, LANES)
     return pl.pallas_call(
         galerkin_kernel,
         out_shape=jax.ShapeDtypeStruct((8, PLANES, 2 * B), F32),
-        in_specs=[scalars] * 5 + [hbm] * 4,
+        in_specs=[hbm] * 9,
         out_specs=pl.BlockSpec(memory_space=pltpu.VMEM),
         scratch_shapes=[
+            pltpu.SMEM((4, ROWS), jnp.int32),
+            pltpu.SMEM((4, ROWS), jnp.int32),
+            pltpu.SMEM((ROWS,), jnp.int32),
+            pltpu.SMEM((32,), jnp.int32),
+            pltpu.SMEM((32,), jnp.int32),
             pltpu.VMEM((ROWS, 4, B, B), BF16),
             pltpu.VMEM((ROWS, B, B), BF16),
             pltpu.VMEM((ROWS, B, B), BF16),
@@ -549,7 +599,9 @@
             pltpu.VMEM((PLANES, 16, LANES), BF16),
             pltpu.VMEM((PLANES * 16, LANES), F32),
             dma((3, PAIRS)),
-            dma,
+            dma((PAIRS,)),
+            dma((5,)),
+            pltpu.SemaphoreType.REGULAR((BITS,)),
             dma((2,)),
             dma((2,)),
             dma((2, PAIRS)),
@@ -564,7 +616,7 @@
             dma((2,)),
         ],
         compiler_params=pltpu.CompilerParams(
-            collective_id=0, has_side_effects=True, vmem_limit_bytes=52 * 1024 * 1024
+            collective_id=0, has_side_effects=True, vmem_limit_bytes=62 * 1024 * 1024
         ),
     )(*operands)
 

time: 142 us -> 134 us (0.944)
  Pallas kernels: 137 us -> 132 us
  local copies, waits for them, and re-layouts: 5.48 us -> 1.77 us
    pallas_call x1, Pallas kernels: 137 us -> 132 us  [galerkin(): pl.pallas_call(galerkin_kernel, out_shape=jax.ShapeDtypeStruct((8, PLANES...]
    unnamed x13 -> x1, local copies, waits for them, and re-layouts: 5.48 us -> 1.77 us
where the time goes in v3:
time: 134 us
  Pallas kernels  132 us (99%)
  local copies, waits for them, and re-layouts  1.77 us (1%)
    pallas_call x1, Pallas kernels, galerkin(): pl.pallas_call(galerkin_kernel, out_shape=jax.ShapeDtypeStruct((8, PLANES...  132 us

profile of v3, /device:TPU:1, one launch (start us, length us, event | category | flops | bytes accessed | tf_op | source)
XLA Modules:
  0.0 134.2 jit_solution(13709071538059153402)
XLA Ops:
  0.0 132.4 %shard_map.91 = f32[8,48,192]{2,1,0:T(8,128)} custom-call(s32[4,64]{1,0:T(4,128)} %bitcast.3, s32[4,64]{1,0:T(4,128)} %bitcast.4, s32[64]{0:T(128)} %label_hbm.1, s32[32]{0:T(128)} %bitcast.5, s32[32]{0:T(128)} %group_hbm.1, bf16[64,4,96,96]{3,2,1,0:T(8,128)(2,1)} %off_hbm.1, bf16[64,96,96]{2,1,0:T(8,128)(2,1)} %diag_hbm.1, bf16[64,96,96]{2,1,0:T(8,128)(2,1)} %inv_hbm.1, ...), custom_call_target="tpu_custom_call" | custom-call | tf_op jit(solution)/shard_map/pallas_call | solution.py:558
  132.4 1.8 %copy.11 = f32[8,48,192]{2,1,0:T(8,128)} copy(f32[8,48,192]{2,1,0:T(8,128)} %shard_map.91) | data formatting | bytes 589824

commit v4 on v3

--- a/solution.py
+++ b/solution.py
@@ -18,7 +18,8 @@
 CHUNKS = 4
 WINDOW = 3
 LAG = 3
-EARLY = 4
+DIRECT = 14
+EARLY = 1
 BITS = 6
 
 
@@ -115,7 +116,7 @@
     group_sem,
 ):
     me = lax.axis_index("col")
-    right, left = lax.rem(me + 1, 4), lax.rem(me + 3, 4)
+    right, left, opposite = [lax.rem(me + d, 4) for d in (1, 3, 2)]
     tile = lax.axis_index("row")
     z = tile // 8
     place = lax.rem(lax.rem(tile, 8) + 32 - 2 * z - 2, 8)
@@ -172,7 +173,7 @@
         return tile + size * (1 - 2 * lax.rem(tile // size, 2))
 
     barrier = pltpu.get_barrier_semaphore()
-    for peer in (left, right):
+    for peer in (left, right, opposite):
         pl.semaphore_signal(barrier, inc=1, device_id={"col": peer}, device_id_type=MESH)
     for b in range(BITS):
         pl.semaphore_signal(barrier, inc=1, device_id={"row": partner(b)}, device_id_type=MESH)
@@ -202,7 +203,7 @@
     def _(p):
         pack_tent(p)
 
-    pl.semaphore_wait(barrier, 2 + BITS)
+    pl.semaphore_wait(barrier, 3 + BITS)
 
     def label_copy(side):
         return remote(
@@ -341,14 +342,15 @@
                 ).astype(BF16)
 
     def ways(p):
-        odd = lax.rem(p, 2)
+        odd = p % 2
         ahead = lax.rem(me + 3 + 2 * odd, 4)
         behind = lax.rem(me + 1 + 2 * odd, 4)
         return ahead, behind
 
-    def far_copy(p):
+    def far_copy(p, direct=False):
         return remote(
-            send_far.at[p], near_far.at[p], c_send.at[0, p], c_recv.at[0, p], ways(p)[0]
+            send_far.at[p], near_far.at[p], c_send.at[0, p], c_recv.at[0, p],
+            opposite if direct else ways(p)[0],
         )
 
     def next_copy(p):
@@ -373,28 +375,29 @@
             send_next[p, t] = (hold_next[p, t] + near_far[p, t].astype(F32)).astype(BF16)
         next_copy(p).start()
 
-    def finish(p):
+    def finish(p, direct=False):
         next_copy(p).wait_recv()
         back_copy(p).wait_recv()
         tiles = [
             hold_own[p, t] + near_next[p, t].astype(F32) + near_back[p, t].astype(F32)
             for t in range(3)
         ]
+        if direct:
+            far_copy(p, True).wait_recv()
+            tiles = [tiles[t] + near_far[p, t].astype(F32) for t in range(3)]
         tiles.append(unpack_last(*tiles))
         for e in range(4):
-            at = (e % 2) * 8 + lax.rem(p, 4) * 2 + e // 2
+            at = (e % 2) * 8 + (p % 4) * 2 + e // 2
             staging[pl.ds(at, PLANES, stride=16), :] = tiles[e]
 
-        @pl.when(lax.rem(p, 4) == 3)
-        def _():
+        def send_planes():
             ch = p // 4
+            send_plane[ch] = staging[...].reshape(PLANES, 16, LANES).astype(BF16)
 
             @pl.loop(0, PLANES)
             def _(d):
                 r = lax.rem(tile + d, PLANES)
                 target = plane_device(r)
-                rows = pl.ds(pl.multiple_of(r * 16, 16), 16)
-                send_plane[ch, r] = staging[rows, :].astype(BF16)
 
                 @pl.when(target != tile)
                 def _():
@@ -406,8 +409,13 @@
                         send_plane.at[ch, r], near_plane.at[ch, tile], plane_recv.at[ch]
                     ).start()
 
-    @pl.loop(0, PAIRS)
-    def _(p):
+        if isinstance(p, int):
+            if p % 4 == 3:
+                send_planes()
+        else:
+            pl.when(lax.rem(p, 4) == 3)(send_planes)
+
+    def products(p, direct=False):
         for side in range(2):
             p_copy(side, p).wait_recv()
         for c in range(2):
@@ -445,24 +453,35 @@
         tiles = share(lax.rem(me + 2, 4))
         for t in range(3):
             send_far[p, t] = tiles[t].astype(BF16)
-        far_copy(p).start()
+        far_copy(p, direct).start()
         tiles = share(behind)
         for t in range(3):
             send_back[p, t] = tiles[t].astype(BF16)
         back_copy(p).start()
 
-        @pl.when(p + WINDOW < PAIRS)
-        def _():
-            for side in range(2):
-                p_copy(side, p + WINDOW).start()
+        if not direct:
+
+            @pl.when(p + WINDOW < PAIRS)
+            def _():
+                for side in range(2):
+                    p_copy(side, p + WINDOW).start()
 
         tiles = share(ahead)
         for t in range(3):
-            hold_next[p, t] = tiles[t]
+            if direct:
+                send_next[p, t] = tiles[t].astype(BF16)
+            else:
+                hold_next[p, t] = tiles[t]
+        if direct:
+            next_copy(p).start()
         tiles = share(me)
         for t in range(3):
             hold_own[p, t] = tiles[t]
 
+    @pl.loop(0, DIRECT)
+    def _(p):
+        products(p)
+
         @pl.when(p >= LAG)
         def _():
             forward(p - LAG)
@@ -471,13 +490,15 @@
         def _():
             finish(p - 2 * LAG)
 
-    @pl.loop(PAIRS - LAG, PAIRS)
-    def _(p):
+    for p in range(DIRECT, PAIRS):
+        products(p, True)
+        if p - LAG < DIRECT:
+            forward(p - LAG)
+        finish(p - 2 * LAG)
+    for p in range(PAIRS - LAG, DIRECT):
         forward(p)
-
-    @pl.loop(PAIRS - 2 * LAG, PAIRS)
-    def _(p):
-        finish(p)
+    for p in range(PAIRS - 2 * LAG, PAIRS):
+        finish(p, p >= DIRECT)
 
     def group_copy(target):
         return along_row(
@@ -541,8 +562,8 @@
         first = final[pl.ds(g, PLANES, stride=16), :]
         second = pltpu.roll(final[pl.ds(8 + g, PLANES, stride=16), :], 96, 1)
         high = lax.broadcasted_iota(jnp.int32, first.shape, 1) >= B
-        out_ref[g, :, 0:LANES] = jnp.where(high, second, first)
-        out_ref[g, :, LANES : 2 * B] = second[:, 0 : 2 * B - LANES]
+        out_ref[g, :, 0:LANES] = jnp.where(high, second, first).astype(BF16)
+        out_ref[g, :, LANES : 2 * B] = second[:, 0 : 2 * B - LANES].astype(BF16)
 
     @pl.when(holds)
     def _():
@@ -557,7 +578,7 @@
     share = (PAIRS, 3, 48, LANES)
     return pl.pallas_call(
         galerkin_kernel,
-        out_shape=jax.ShapeDtypeStruct((8, PLANES, 2 * B), F32),
+        out_shape=jax.ShapeDtypeStruct((8, PLANES, 2 * B), BF16),
         in_specs=[hbm] * 9,
         out_specs=pl.BlockSpec(memory_space=pltpu.VMEM),
         scratch_shapes=[
@@ -642,7 +663,7 @@
         diag_blocks,
         diag_inverse,
         tentative,
-    )
+    ).astype(F32)
 
 
 def solution(mesh):

time: 134 us -> 133 us (level)
  local copies, waits for them, and re-layouts: 1.77 us -> 0 us
  other arithmetic: 0 us -> 1.7 us
    unnamed x1 -> x0, local copies, waits for them, and re-layouts: 1.77 us -> none
    convert_element_type x0 -> x1, other arithmetic: none -> 1.7 us  [on_device(): return galerkin(neighbour.T, active.T, aggregate, owner_row[:, 0], owner_...]
where the time goes in v4:
time: 133 us
  Pallas kernels  131 us (98%)
  other arithmetic  1.7 us (1%)
    pallas_call x1, Pallas kernels, galerkin(): pl.pallas_call(galerkin_kernel, out_shape=jax.ShapeDtypeStruct((8, PLANES...  131 us

profile of v4, /device:TPU:1, one launch (start us, length us, event | category | flops | bytes accessed | tf_op | source)
XLA Modules:
  0.0 133.2 jit_solution(15093961084352792280)
XLA Ops:
  0.0 131.5 %shard_map.91 = bf16[8,48,192]{2,1,0:T(8,128)(2,1)} custom-call(s32[4,64]{1,0:T(4,128)} %bitcast.3, s32[4,64]{1,0:T(4,128)} %bitcast.4, s32[64]{0:T(128)} %label_hbm.1, s32[32]{0:T(128)} %bitcast.5, s32[32]{0:T(128)} %group_hbm.1, bf16[64,4,96,96]{3,2,1,0:T(8,128)(2,1)} %off_hbm.1, bf16[64,96,96]{2,1,0:T(8,128)(2,1)} %diag_hbm.1, ...), custom_call_target="tpu_custom_call" | custom-call | tf_op jit(solution)/shard_map/pallas_call | solution.py:579
  131.5 1.7 %convert_element_type.3 = f32[8,48,192]{2,1,0:T(8,128)} convert(bf16[8,48,192]{2,1,0:T(8,128)(2,1)} %shard_map.91) | non-fusion elementwise | flops 73728 | bytes 442368 | tf_op jit(solution)/shard_map/convert_element_type | solution.py:666

commit v5 on v4

--- a/solution.py
+++ b/solution.py
@@ -71,8 +71,10 @@
     inv,
     tent,
     wide,
+    own_label,
+    near_label,
     send_label,
-    near_label,
+    got_label,
     send_t,
     near_t,
     own_p,
@@ -189,7 +191,13 @@
 
     @pl.loop(0, ROWS)
     def _(f):
-        send_label[pl.ds(f, 1), :] = jnp.full((1, LANES), label_smem[f], jnp.int32).astype(F32)
+        own_label[pl.ds(f, 1), :] = jnp.full((1, LANES), label_smem[f], jnp.int32).astype(F32)
+
+    here = lax.broadcasted_iota(jnp.int32, (ROWS, LANES), 0) == lax.broadcasted_iota(
+        jnp.int32, (ROWS, LANES), 1
+    )
+    line = jnp.sum(jnp.where(here, own_label[...], 0.0), axis=0, keepdims=True)
+    send_label[...] = jnp.broadcast_to(line, (8, LANES))
 
     def pack_tent(p):
         tent_load(p).wait()
@@ -207,7 +215,7 @@
 
     def label_copy(side):
         return remote(
-            send_label, near_label.at[side], label_send.at[side], label_recv.at[side],
+            send_label, got_label.at[side], label_send.at[side], label_recv.at[side],
             right if side == 0 else left,
         )
 
@@ -261,8 +269,8 @@
     lane = lax.broadcasted_iota(jnp.int32, (8, LANES), 1)
     mine = jnp.zeros((8, LANES), jnp.int32)
     for q in range(32):
-        here = (sub == q // 8) & (lane == lax.rem(tile, 16) * 8 + q % 8)
-        mine = jnp.where(here, owner_smem[q] * 8 + group_smem[q], mine)
+        place_of = (sub == q // 8) & (lane == lax.rem(tile, 16) * 8 + q % 8)
+        mine = jnp.where(place_of, owner_smem[q] * 8 + group_smem[q], mine)
     send_target[...] = mine
 
     @pl.loop(0, PLANES)
@@ -279,6 +287,10 @@
 
     for side in range(2):
         label_copy(side).wait_recv()
+        column = jnp.sum(
+            jnp.where(here, got_label[side, 0:1, :], 0.0), axis=1, keepdims=True
+        )
+        near_label[side] = jnp.broadcast_to(column, (ROWS, LANES))
 
     def apply(row, near_base, own):
         total = dot(diag[row], rim[near_base + own])
@@ -307,7 +319,7 @@
             for e in range(4):
                 spread(e, 4 * side, tiles[e], near_label[side, pl.ds(p * 4 + e, 1), :])
         for e in range(4):
-            spread(e, 2, wide[p * 4 + e].astype(F32), send_label[pl.ds(p * 4 + e, 1), :])
+            spread(e, 2, wide[p * 4 + e].astype(F32), own_label[pl.ds(p * 4 + e, 1), :])
 
         for c in range(2):
             blocks = []
@@ -594,6 +606,8 @@
             pltpu.VMEM((ROWS, B, LANES), BF16),
             pltpu.VMEM((ROWS, LANES), F32),
             pltpu.VMEM((2, ROWS, LANES), F32),
+            pltpu.VMEM((8, LANES), F32),
+            pltpu.VMEM((2, 8, LANES), F32),
             pltpu.VMEM((PAIRS, 3, B, LANES), BF16),
             pltpu.VMEM((2, PAIRS, 3, B, LANES), BF16),
             pltpu.VMEM((ROWS, B, 2 * LANES), BF16),

time: 133 us -> 133 us (level)
  no operation moved by 1% of the time
where the time goes in v5:
time: 133 us
  Pallas kernels  131 us (98%)
  other arithmetic  1.7 us (1%)
    pallas_call x1, Pallas kernels, galerkin(): pl.pallas_call(galerkin_kernel, out_shape=jax.ShapeDtypeStruct((8, PLANES...  131 us

profile of v5, /device:TPU:1, one launch (start us, length us, event | category | flops | bytes accessed | tf_op | source)
XLA Modules:
  0.0 132.9 jit_solution(8958560504575363810)
XLA Ops:
  0.0 131.2 %shard_map.91 = bf16[8,48,192]{2,1,0:T(8,128)(2,1)} custom-call(s32[4,64]{1,0:T(4,128)} %bitcast.3, s32[4,64]{1,0:T(4,128)} %bitcast.4, s32[64]{0:T(128)} %label_hbm.1, s32[32]{0:T(128)} %bitcast.5, s32[32]{0:T(128)} %group_hbm.1, bf16[64,4,96,96]{3,2,1,0:T(8,128)(2,1)} %off_hbm.1, bf16[64,96,96]{2,1,0:T(8,128)(2,1)} %diag_hbm.1, ...), custom_call_target="tpu_custom_call" | custom-call | tf_op jit(solution)/shard_map/pallas_call | solution.py:591
  131.2 1.7 %convert_element_type.3 = f32[8,48,192]{2,1,0:T(8,128)} convert(bf16[8,48,192]{2,1,0:T(8,128)(2,1)} %shard_map.91) | non-fusion elementwise | flops 73728 | bytes 442368 | tf_op jit(solution)/shard_map/convert_element_type | solution.py:680
